TPU v7x, 32 devices: a whole 2x2x4 slice. The times are simulated.
32 devices in a mesh: rep: 8 (over z, x), fsdp: 4 (over y, core).
Axes of the slice: x: 2, y: 2, z: 4, core: 2. Of those that a mesh axis runs over, the one named last changes fastest.
Arguments:
- hidden: bfloat16 [8, 1024, 4608], P('rep', 'fsdp'), may hold values from -6 to 6
- upstream: bfloat16 [8, 1024, 1024], P('rep', 'fsdp'), may hold values from -6 to 6
- weights: bfloat16 [8, 4608, 1024], P('rep', 'fsdp'), may hold values from -6 to 6
- moment_one: bfloat16 [8, 4608, 1024], P('rep', 'fsdp'), may hold values from -0.59765625 to 0.59765625
- moment_two: bfloat16 [8, 4608, 1024], P('rep', 'fsdp'), may hold values from 0.0029907227 to 0.099609375
- global_params: float32 [4, 1152, 1024], P('fsdp', 'rep'), may hold values from -6 to 6
- outer_momentum: float32 [4, 1152, 1024], P('fsdp', 'rep'), may hold values from -2 to 2
Outputs:
- values: bfloat16 [8, 1024, 1024], P('rep', 'fsdp')
- merged: bfloat16 [8, 4608, 1024], P('rep', 'fsdp')
- new_global: float32 [4, 1152, 1024], P('fsdp', 'rep')
- new_momentum: float32 [4, 1152, 1024], P('fsdp', 'rep')
All inputs are finite; a program needn't handle non-finite values.
Results may differ from a plain program's by a relative error of at most 0.007.
Values may be sent and summed in bfloat16 or wider, within the bound.
A program may use at most 128 MiB of HBM per device.

v0:
```python
import jax
import jax.numpy as jnp
from jax import lax
from jax.sharding import PartitionSpec as P

beta_one = 0.9
beta_two = 0.95
bias_one = 1.0 - 0.9**8
bias_two = 1.0 - 0.95**8
inner_rate = 0.25
decay_rate = 0.1
epsilon = 1e-08
outer_rate = 0.7
outer_mu = 0.9
mixing = 0.5


def on_device(hidden, upstream, weights, moment_one, moment_two, global_params, outer_momentum):
    factor = float(hidden.shape[2]) ** (-0.5)
    tokens = hidden[0]
    grads_in = upstream[0]
    local_rows = weights[0]
    selected = tokens
    projected = jnp.dot(
        selected,
        lax.all_gather(weights, "fsdp", axis=1, tiled=True)[0],
        preferred_element_type=jnp.float32,
    )
    values = (projected * factor).astype(jnp.bfloat16)
    selected = tokens
    gradient = lax.psum_scatter(
        (
            lax.dot_general(
                selected, grads_in, (((0,), (0,)), ((), ())), preferred_element_type=jnp.float32
            )
            * factor
        ).astype(jnp.bfloat16),
        "fsdp",
        scatter_dimension=0,
        tiled=True,
    ).astype(jnp.float32)
    moment_new = beta_one * moment_one[0].astype(jnp.float32) + (1.0 - beta_one) * gradient
    second_new = (
        beta_two * moment_two[0].astype(jnp.float32) + (1.0 - beta_two) * gradient * gradient
    )
    stepped = moment_new / bias_one / (jnp.sqrt(second_new / bias_two) + epsilon)
    current = local_rows.astype(jnp.float32)
    updated = current - inner_rate * (stepped + decay_rate * current)
    summed = lax.psum(weights.astype(jnp.float32), "rep")
    owned_rows = global_params.shape[1]
    owned = lax.dynamic_slice_in_dim(summed, lax.axis_index("rep") * owned_rows, owned_rows, 1)
    pseudo = global_params - owned / lax.axis_size("rep")
    momentum = outer_mu * outer_momentum + pseudo
    renewed = global_params - outer_rate * (pseudo + outer_mu * momentum)
    spread = lax.all_gather(renewed.astype(jnp.bfloat16), "rep", axis=1, tiled=True).astype(
        renewed.dtype
    )[0]
    merged = (mixing * updated + (1.0 - mixing) * spread).astype(jnp.bfloat16)
    return (values[None], merged[None], renewed, momentum)


def solution(mesh):
    return jax.shard_map(
        on_device,
        mesh=mesh,
        in_specs=(
            P("rep", "fsdp", None),
            P("rep", "fsdp", None),
            P("rep", "fsdp", None),
            P("rep", "fsdp", None),
            P("rep", "fsdp", None),
            P("fsdp", "rep", None),
            P("fsdp", "rep", None),
        ),
        out_specs=(
            P("rep", "fsdp", None),
            P("rep", "fsdp", None),
            P("fsdp", "rep", None),
            P("fsdp", "rep", None),
        ),
        check_vma=False,
    )
```

profile of v0, /device:TPU:9, one launch (start us, length us, event | category | flops | bytes accessed | tf_op | source)
XLA Modules:
  0.0 343.3 jit_solution(15229346544464123296)
XLA Ops:
  7.2 0.0 copy-start
  7.2 0.0 copy-start.1
  7.2 0.0 copy-start.2
  7.2 0.0 all-gather.3.cloned.1.call-start
  7.2 0.7 all-gather.3.cloned.1.call-update
  7.9 0.0 all-gather.5.cloned.1.call-start
  8.0 185.1 %all-reduce.1 = f32[1,1152,1024]{2,1,0:T(8,128)} all-reduce(bf16[1,1152,1024]{2,1,0:T(8,128)(2,1)} %param.9), channel_id=1, replica_groups=mesh['rep'=8,'fsdp'=4] {'rep'}, use_global_device_ids=true, to_apply=%region_1.0 | all-reduce | flops 1179648 | bytes 7077888 | tf_op jit(solution)/shard_map/psum | solution.py:49
  193.1 0.0 copy-done.1
  193.1 0.0 copy-done.2
  193.1 2.4 fusion.32
  195.5 0.0 all-gather.5.cloned.1.call-update
  195.5 0.0 reduce-scatter.2.cloned.1.call-start
  195.6 0.0 copy-done
  195.6 6.1 %multiply_convert_fusion = bf16[4608,1024]{1,0:T(8,128)(2,1)} fusion(bf16[1,256,4608]{2,1,0:T(8,128)(2,1)S(1)} %copy-done, bf16[1,256,1024]{2,1,0:T(8,128)(2,1)} %param.8), kind=kOutput, calls=%fused_computation | convolution fusion | flops 2425356288 | bytes 12320768 | tf_op jit(solution)/shard_map/dot_general | solution.py:33
  201.7 0.0 reduce-scatter.2.cloned.1.call-update
  201.7 0.0 all-gather.3.cloned.1.call-done
  201.8 7.2 %fusion.26 = bf16[1,256,1024]{2,1,0:T(8,128)(2,1)} fusion(bf16[1,4608,1024]{2,1,0:T(8,128)(2,1)} %all-gather.3.cloned.1.call-done, bf16[1,256,4608]{2,1,0:T(8,128)(2,1)S(1)} %copy-done), kind=kOutput, calls=%fused_computation.23 | convolution fusion | flops 2416443392 | bytes 12320768 | tf_op jit(solution)/shard_map/dot_general | solution.py:24
  209.0 38.5 %all-gather.5.cloned.1.call-done = bf16[1,1152,1024]{2,1,0:T(8,128)(2,1)} async-done(((bf16[1,144,1024]{2,1,0:T(8,128)(2,1)}), bf16[1,1152,1024]{2,1,0:T(8,128)(2,1)}) %all-gather.5.cloned.1.call-update) | async-done | bytes 2359312 | tf_op jit(solution)/shard_map/all_gather | solution.py:55
  247.5 80.7 %reduce-scatter.2.cloned.1.call-done = bf16[1152,1024]{1,0:T(8,128)(2,1)} async-done(((bf16[4608,1024]{1,0:T(8,128)(2,1)}), bf16[1152,1024]{1,0:T(8,128)(2,1)}) %reduce-scatter.2.cloned.1.call-update) | async-done | bytes 2359312 | tf_op jit(solution)/shard_map/reduce_scatter | solution.py:31
  328.2 8.6 %fusion.15 = bf16[1,1152,1024]{2,1,0:T(8,128)(2,1)} fusion(bf16[1,1152,1024]{2,1,0:T(8,128)(2,1)} %all-gather.5.cloned.1.call-done, bf16[1,1152,1024]{2,1,0:T(8,128)(2,1)} %param.11, bf16[1152,1024]{1,0:T(8,128)(2,1)} %reduce-scatter.2.cloned.1.call-done, bf16[1,1152,1024]{2,1,0:T(8,128)(2,1)} %param.10, bf16[1,1152,1024]{2,1,0:T(8,128)(2,1)} %param.9), kind=kLoop, calls=%fused_computation.20 | loop fusion | flops 27131904 | bytes 14155776 | tf_op jit(solution)/shard_map/broadcast_in_dim | solution.py:59
Async XLA Ops:
  7.2 188.4 %copy-start = (bf16[1,256,4608]{2,1,0:T(8,128)(2,1)S(1)}, bf16[1,256,4608]{2,1,0:T(8,128)(2,1)}, u32[]{:S(2)}) copy-start(bf16[1,256,4608]{2,1,0:T(8,128)(2,1)} %param.7) | copy-start | bytes 7077892
  7.2 185.9 %copy-start.1 = (f32[1,144,1024]{2,1,0:T(8,128)S(1)}, f32[1,144,1024]{2,1,0:T(8,128)}, u32[]{:S(2)}) copy-start(f32[1,144,1024]{2,1,0:T(8,128)} %param.12) | copy-start | bytes 1769476
  7.2 185.9 %copy-start.2 = (f32[1,144,1024]{2,1,0:T(8,128)S(1)}, f32[1,144,1024]{2,1,0:T(8,128)}, u32[]{:S(2)}) copy-start(f32[1,144,1024]{2,1,0:T(8,128)} %param.13) | copy-start | bytes 1769476
  7.2 194.6 %all-gather.3.cloned.1.call-start = ((), (), s32[]{:S(2)}) async-start(), calls=%async_computation.1 | async-start | bytes 11796480 | tf_op jit(solution)/shard_map/all_gather | solution.py:26
  7.9 239.6 %all-gather.5.cloned.1.call-start = ((), (), s32[]{:S(2)}) async-start(), calls=%async_computation.3 | async-start | bytes 2654208 | tf_op jit(solution)/shard_map/all_gather | solution.py:55
  195.5 132.7 %reduce-scatter.2.cloned.1.call-start = ((), (), s32[]{:S(2)}) async-start(), calls=%async_computation.2 | async-start | bytes 11796480 | tf_op jit(solution)/shard_map/reduce_scatter | solution.py:31
Sparse Core Ops, SparseCore 0:
  9.6 65.8 all-gather.2
  195.6 51.8 all-gather.4
  250.1 78.0 reduce-scatter.1
where the time goes:
time: 345 us; the launch traced here: 343 us
  blocking collectives  185 us (54%)
  waiting for transfers between devices  120 us (35%)
  between operations  13.8 us (4%)
  matrix products  13.4 us (4%)
  other arithmetic  11 us (3%)
    psum x1, blocking collectives, on_device(): summed = lax.psum(weights.astype(jnp.float32), 'rep')  185 us
    reduce_scatter x1, waiting for transfers between devices, on_device(): lax.psum_scatter((lax.dot_general(selected, grads_in, (((0,), (0,)), ((),...  80.7 us
    all_gather x1, waiting for transfers between devices, on_device(): lax.all_gather(renewed.astype(jnp.bfloat16), 'rep', axis=1, tiled=True)  38.5 us
    broadcast_in_dim x1, other arithmetic, on_device(): return (values[None], merged[None], renewed, momentum)  8.61 us
    dot_general x1, matrix products, on_device(): jnp.dot(selected, lax.all_gather(weights, 'fsdp', axis=1, tiled=True)[0],...  7.25 us
  transfers between devices with their start and end apart: 3, of which 2 were waited for; matrix products, arithmetic and copies ran while one was open for 5% of the time, Pallas kernels for 0%

commit v1 on v0

v1 whole, which is shorter than its diff:
```python
import functools

import jax
import jax.numpy as jnp
from jax import lax
from jax.experimental import pallas as pl
from jax.experimental.pallas import tpu as pltpu
from jax.sharding import PartitionSpec as P

beta_one = 0.9
beta_two = 0.95
bias_one = 1.0 - 0.9**8
bias_two = 1.0 - 0.95**8
inner_rate = 0.25
decay_rate = 0.1
epsilon = 1e-08
outer_rate = 0.7
outer_mu = 0.9
mixing = 0.5

MESH = pl.DeviceIdType.MESH
BF16 = jnp.bfloat16
F32 = jnp.float32
HALVES = 2
STRIP = 16


def inner_step(gradient, first, second, current):
    moment_new = beta_one * first + (1.0 - beta_one) * gradient
    second_new = beta_two * second + (1.0 - beta_two) * gradient * gradient
    stepped = moment_new / bias_one / (jnp.sqrt(second_new / bias_two) + epsilon)
    return current - inner_rate * (stepped + decay_rate * current)


def strips(rows, body):
    @pl.loop(0, rows // STRIP)
    def _(i):
        body(pl.multiple_of(i * STRIP, STRIP))


def fused(
    reps,
    hidden, upstream, weights, moment_one, moment_two, global_params, outer_momentum,
    values_out, merged_out, renewed_out, momentum_out,
    h_all, u_all, w, m1, m2, g, om,
    x_in, z_out, z_in, acc, spread, grad, p_own, p_out, p_in, y_out, y_in,
    val, mer, ren, mom,
    local_sem, store_sem, merged_sem,
    h_send, h_recv, u_send, u_recv, p_send, p_recv,
    x_send, x_recv, z_send, z_recv, gz_send, gz_recv, gx_send, gx_recv,
):
    tokens, width = hidden.shape[1:]
    block, columns = weights.shape[1:]
    rows = block // reps
    layers = reps // 2
    half = columns // HALVES
    factor = float(width) ** (-0.5)

    me_rep = lax.axis_index("rep")
    me_shard = lax.axis_index("fsdp")
    z, x = me_rep // 2, me_rep % 2
    y, core = me_shard // 2, me_shard % 2
    sibling = y * 2 + (1 - core)
    across = (1 - y) * 2 + core
    diagonal = (1 - y) * 2 + (1 - core)
    shards = (me_shard, sibling, across, diagonal)
    x_peer = z * 2 + (1 - x)

    def layer(d):
        return (z + d + layers) % layers

    def at_shard(p):
        return (me_rep, p)

    def at_rep(r):
        return (r, me_shard)

    def row_block(owner):
        return pl.ds(pl.multiple_of(owner * rows, STRIP), rows)

    def cols(h):
        return pl.ds(h * half, half)

    def toks(j):
        return pl.ds(j * tokens, tokens)

    def remote(src, dst, send, recv, device):
        return pltpu.make_async_remote_copy(
            src_ref=src, dst_ref=dst, send_sem=send, recv_sem=recv,
            device_id=device, device_id_type=MESH,
        )

    loads = [
        (hidden.at[0, :, pl.ds(pl.multiple_of(me_shard * block, 128), block)], h_all.at[toks(0)]),
        (weights.at[0], w),
        (upstream.at[0], u_all.at[toks(0)]),
        (global_params.at[0], g),
        (outer_momentum.at[0], om),
        (moment_one.at[0], m1),
        (moment_two.at[0], m2),
    ]
    loads = [pltpu.make_async_copy(a, b, local_sem.at[i]) for i, (a, b) in enumerate(loads)]
    for copy in loads:
        copy.start()

    barrier = pltpu.get_barrier_semaphore()
    greeted = [at_shard(p) for p in shards[1:]] + [at_rep(x_peer)]
    greeted += [at_rep(layer(d) * 2 + x) for d in range(1, layers)]
    for device in greeted:
        pl.semaphore_signal(barrier, inc=1, device_id=device, device_id_type=MESH)
    pl.semaphore_wait(barrier, len(greeted))

    sent = []

    def go(copy):
        copy.start()
        sent.append(copy)

    def send_hidden(j):
        part = hidden.at[0, :, pl.ds(pl.multiple_of(shards[j] * block, 128), block)]
        go(remote(part, h_all.at[toks(j)], h_send.at[j - 1], h_recv.at[j - 1], at_shard(shards[j])))

    def hidden_in(j):
        dst = h_all.at[toks(j)]
        remote(dst, dst, h_send.at[j - 1], h_recv.at[j - 1], at_shard(shards[j])).wait_recv()

    def send_upstream(j):
        go(remote(upstream.at[0], u_all.at[toks(j)], u_send.at[j - 1], u_recv.at[j - 1], at_shard(shards[j])))

    def upstream_in(j):
        dst = u_all.at[toks(j)]
        remote(dst, dst, u_send.at[j - 1], u_recv.at[j - 1], at_shard(shards[j])).wait_recv()

    order = tuple(range(1, layers)) + (0,)
    send_hidden(3)
    send_hidden(2)
    for h in range(HALVES):
        for d in order:
            part = weights.at[0, row_block(layer(d) * 2 + (1 - x)), cols(h)]
            go(remote(part, x_in.at[d, :, cols(h)], x_send.at[h, d], x_recv.at[h, d], at_rep(x_peer)))
    send_hidden(1)
    send_upstream(1)
    send_upstream(2)

    def project(j, dst):
        @pl.loop(0, columns // 256)
        def _(n):
            at = pl.ds(pl.multiple_of(n * 256, 256), 256)
            dst[:, at] = jnp.dot(h_all[toks(j), :], w[:, at], preferred_element_type=F32)

    loads[0].wait()
    loads[1].wait()
    project(0, p_own)
    hidden_in(1)
    project(1, p_out.at[0])
    go(remote(p_out.at[0], p_in.at[0], p_send.at[0], p_recv.at[0], at_shard(sibling)))

    for h in range(HALVES):
        for d in order:
            dst = x_in.at[d, :, cols(h)]
            remote(dst, dst, x_send.at[h, d], x_recv.at[h, d], at_rep(x_peer)).wait_recv()
            base = (layer(d) * 2 + x) * rows

            def pair(i, d=d, h=h, base=base):
                here = pl.ds(pl.multiple_of(base + i, STRIP), STRIP)
                total = w[here, cols(h)].astype(F32) + x_in[d, pl.ds(i, STRIP), cols(h)].astype(F32)
                if d == 0:
                    acc[pl.ds(i, STRIP), cols(h)] = total
                else:
                    z_out[d - 1, pl.ds(i, STRIP), cols(h)] = total.astype(BF16)

            strips(rows, pair)
            if d:
                go(remote(
                    z_out.at[d - 1, :, cols(h)], z_in.at[d - 1, :, cols(h)],
                    z_send.at[h, d - 1], z_recv.at[h, d - 1], at_rep(layer(d) * 2 + x),
                ))

    loads[3].wait()
    loads[4].wait()
    stores = []
    for h in range(HALVES):
        for d in range(1, layers):
            dst = z_in.at[d - 1, :, cols(h)]
            remote(dst, dst, z_send.at[h, d - 1], z_recv.at[h, d - 1], at_rep(me_rep)).wait_recv()

        def outer(i, h=h):
            here = pl.ds(i, STRIP)
            summed = acc[here, cols(h)]
            for d in range(1, layers):
                summed = summed + z_in[d - 1, here, cols(h)].astype(F32)
            now = g[here, cols(h)]
            pseudo = now - summed / reps
            momentum = outer_mu * om[here, cols(h)] + pseudo
            renewed = now - outer_rate * (pseudo + outer_mu * momentum)
            mom[here, cols(h)] = momentum
            ren[here, cols(h)] = renewed
            at = pl.ds(pl.multiple_of(me_rep * rows + i, STRIP), STRIP)
            spread[at, cols(h)] = renewed.astype(BF16)

        strips(rows, outer)
        own = spread.at[row_block(me_rep), cols(h)]
        go(remote(own, own, gx_send.at[h, 0], gx_recv.at[h, 0], at_rep(x_peer)))
        for d in order[:-1]:
            go(remote(own, own, gz_send.at[h, d - 1], gz_recv.at[h, d - 1], at_rep(layer(d) * 2 + x)))
    stores.append(pltpu.make_async_copy(ren, renewed_out.at[0], store_sem.at[0]))
    stores.append(pltpu.make_async_copy(mom, momentum_out.at[0], store_sem.at[1]))
    stores[0].start()
    stores[1].start()

    hidden_in(3)
    project(3, p_out.at[1])
    go(remote(p_out.at[1], p_in.at[1], p_send.at[1], p_recv.at[1], at_shard(sibling)))
    hidden_in(2)

    @pl.loop(0, columns // 256)
    def _(n):
        at = pl.ds(pl.multiple_of(n * 256, 256), 256)
        grad[pl.ds(0, tokens), at] = jnp.dot(h_all[toks(2), :], w[:, at], preferred_element_type=F32)

    remote(p_in.at[1], p_in.at[1], p_send.at[1], p_recv.at[1], at_shard(sibling)).wait_recv()

    def chip_sum(i):
        here = pl.ds(i, STRIP)
        y_out[here, :] = (grad[here, :] + p_in[1, here, :]).astype(BF16)

    strips(tokens, chip_sum)
    go(remote(y_out, y_in, p_send.at[2], p_recv.at[2], at_shard(across)))

    def forward(h, d):
        part = spread.at[row_block(layer(-d) * 2 + x), cols(h)]
        remote(part, part, gz_send.at[h, d - 1], gz_recv.at[h, d - 1], at_rep(me_rep)).wait_recv()
        go(remote(part, part, gx_send.at[h, d], gx_recv.at[h, d], at_rep(x_peer)))

    upstream_in(2)
    go(remote(u_all.at[toks(2)], u_all.at[toks(3)], u_send.at[2], u_recv.at[2], at_shard(sibling)))
    near_first = (1,) + tuple(range(layers - 1, 1, -1))
    for d in near_first:
        forward(0, d)
    loads[2].wait()
    loads[5].wait()
    loads[6].wait()
    upstream_in(1)
    upstream_in(3)

    part_rows = block // 3

    def inner(part):
        lhs = h_all[:, pl.ds(part * part_rows, part_rows)]
        base = part * part_rows

        @pl.loop(0, columns // 256)
        def _(n):
            at = pl.ds(pl.multiple_of(n * 256, 256), 256)
            grad[pl.ds(base, part_rows), at] = lax.dot_general(
                lhs, u_all[:, at], (((0,), (0,)), ((), ())), preferred_element_type=F32
            )

        def step(i):
            here = pl.ds(pl.multiple_of(base + i, STRIP), STRIP)
            updated = inner_step(
                grad[here, :] * factor, m1[here, :].astype(F32), m2[here, :].astype(F32), w[here, :].astype(F32)
            )
            grad[here, :] = mixing * updated

        strips(part_rows, step)

    inner(0)
    for d in near_first:
        forward(1, d)
    inner(1)
    inner(2)

    remote(p_in.at[0], p_in.at[0], p_send.at[0], p_recv.at[0], at_shard(sibling)).wait_recv()
    remote(y_in, y_in, p_send.at[2], p_recv.at[2], at_shard(across)).wait_recv()

    def finish(i):
        here = pl.ds(i, STRIP)
        total = p_own[here, :] + p_in[0, here, :] + y_in[here, :].astype(F32)
        val[here, :] = (total * factor).astype(BF16)

    strips(tokens, finish)
    stores.append(pltpu.make_async_copy(val, values_out.at[0], store_sem.at[2]))
    stores[2].start()

    def merge(owner, slot):
        base = owner * rows

        def body(i):
            here = pl.ds(pl.multiple_of(base + i, STRIP), STRIP)
            mer[here, :] = (grad[here, :] + (1.0 - mixing) * spread[here, :].astype(F32)).astype(BF16)

        strips(rows, body)
        copy = pltpu.make_async_copy(
            mer.at[row_block(owner)], merged_out.at[0, row_block(owner)], merged_sem.at[slot]
        )
        copy.start()
        stores.append(copy)

    merge(me_rep, 0)
    for i, d in enumerate(near_first):
        merge(layer(-d) * 2 + x, i + 1)
    for i, d in enumerate((0,) + near_first):
        owner = layer(-d) * 2 + (1 - x)
        for h in range(HALVES):
            part = spread.at[row_block(owner), cols(h)]
            remote(part, part, gx_send.at[h, d], gx_recv.at[h, d], at_rep(x_peer)).wait_recv()
        merge(owner, layers + i)

    for copy in sent:
        copy.wait_send()
    for copy in stores:
        copy.wait()


def fused_call(reps, hidden, upstream, weights, moment_one, moment_two, global_params, outer_momentum):
    tokens = hidden.shape[1]
    block, columns = weights.shape[1:]
    rows = block // reps
    layers = reps // 2
    dma = pltpu.SemaphoreType.DMA
    scratch = [
        pltpu.VMEM((4 * tokens, block), BF16),
        pltpu.VMEM((4 * tokens, columns), BF16),
        pltpu.VMEM((block, columns), BF16),
        pltpu.VMEM((block, columns), BF16),
        pltpu.VMEM((block, columns), BF16),
        pltpu.VMEM((rows, columns), F32),
        pltpu.VMEM((rows, columns), F32),
        pltpu.VMEM((layers, rows, columns), BF16),
        pltpu.VMEM((layers - 1, rows, columns), BF16),
        pltpu.VMEM((layers - 1, rows, columns), BF16),
        pltpu.VMEM((rows, columns), F32),
        pltpu.VMEM((block, columns), BF16),
        pltpu.VMEM((block, columns), F32),
        pltpu.VMEM((tokens, columns), F32),
        pltpu.VMEM((2, tokens, columns), F32),
        pltpu.VMEM((2, tokens, columns), F32),
        pltpu.VMEM((tokens, columns), BF16),
        pltpu.VMEM((tokens, columns), BF16),
        pltpu.VMEM((tokens, columns), BF16),
        pltpu.VMEM((block, columns), BF16),
        pltpu.VMEM((rows, columns), F32),
        pltpu.VMEM((rows, columns), F32),
        dma((7,)), dma((3,)), dma((reps,)),
        dma((3,)), dma((3,)), dma((3,)), dma((3,)), dma((3,)), dma((3,)),
        dma((HALVES, layers)), dma((HALVES, layers)),
        dma((HALVES, layers - 1)), dma((HALVES, layers - 1)),
        dma((HALVES, layers - 1)), dma((HALVES, layers - 1)),
        dma((HALVES, layers)), dma((HALVES, layers)),
    ]
    anywhere = pl.BlockSpec(memory_space=pl.ANY)
    return pl.pallas_call(
        functools.partial(fused, reps),
        out_shape=(
            jax.ShapeDtypeStruct((1, tokens, columns), BF16),
            jax.ShapeDtypeStruct(weights.shape, BF16),
            jax.ShapeDtypeStruct(global_params.shape, F32),
            jax.ShapeDtypeStruct(global_params.shape, F32),
        ),
        in_specs=[anywhere] * 7,
        out_specs=[anywhere] * 4,
        scratch_shapes=scratch,
        compiler_params=pltpu.CompilerParams(
            collective_id=0, has_side_effects=True, vmem_limit_bytes=56 * 1024 * 1024
        ),
        cost_estimate=pl.CostEstimate(
            flops=4 * tokens * hidden.shape[2] * columns, bytes_accessed=18 * 1024 * 1024, transcendentals=0
        ),
    )(hidden, upstream, weights, moment_one, moment_two, global_params, outer_momentum)


def collective_form(hidden, upstream, weights, moment_one, moment_two, global_params, outer_momentum):
    factor = float(hidden.shape[2]) ** (-0.5)
    tokens, grads_in = hidden[0], upstream[0]
    gathered = lax.all_gather(weights, "fsdp", axis=1, tiled=True)[0]
    values = (jnp.dot(tokens, gathered, preferred_element_type=F32) * factor).astype(BF16)
    partial = lax.dot_general(tokens, grads_in, (((0,), (0,)), ((), ())), preferred_element_type=F32)
    gradient = lax.psum_scatter(
        (partial * factor).astype(BF16), "fsdp", scatter_dimension=0, tiled=True
    ).astype(F32)
    updated = inner_step(
        gradient, moment_one[0].astype(F32), moment_two[0].astype(F32), weights[0].astype(F32)
    )
    owned = lax.psum_scatter(weights.astype(F32), "rep", scatter_dimension=1, tiled=True)
    pseudo = global_params - owned / lax.axis_size("rep")
    momentum = outer_mu * outer_momentum + pseudo
    renewed = global_params - outer_rate * (pseudo + outer_mu * momentum)
    spread = lax.all_gather(renewed.astype(BF16), "rep", axis=1, tiled=True).astype(F32)[0]
    merged = (mixing * updated + (1.0 - mixing) * spread).astype(BF16)
    return (values[None], merged[None], renewed, momentum)


def solution(mesh):
    reps, shards = mesh.shape["rep"], mesh.shape["fsdp"]

    def on_device(*arrays):
        rows = arrays[5].shape[1]
        if shards == 4 and reps % 2 == 0 and reps > 2 and rows % STRIP == 0:
            return fused_call(reps, *arrays)
        return collective_form(*arrays)

    return jax.shard_map(
        on_device,
        mesh=mesh,
        in_specs=(P("rep", "fsdp", None),) * 5 + (P("fsdp", "rep", None),) * 2,
        out_specs=(P("rep", "fsdp", None),) * 2 + (P("fsdp", "rep", None),) * 2,
        check_vma=False,
    )
```

time: 345 us -> 81.6 us (0.24)
  blocking collectives: 185 us -> 0 us
  waiting for transfers between devices: 120 us -> 0 us
  Pallas kernels: 0 us -> 73.6 us
  matrix products: 13.4 us -> 0 us
  between operations: 13.8 us -> 0.64 us
  other arithmetic: 11 us -> 0 us
  local copies, waits for them, and re-layouts: 0.02 us -> 6.87 us
    psum x1 -> x0, blocking collectives: 185 us -> none  [on_device(): summed = lax.psum(weights.astype(jnp.float32), 'rep')]
    reduce_scatter x1 -> x0, waiting for transfers between devices: 80.7 us -> none  [on_device(): lax.psum_scatter((lax.dot_general(selected, grads_in, (((0,), (0,)), ((),...]
    pallas_call x0 -> x1, Pallas kernels: none -> 73.6 us  [fused_call(): pl.pallas_call(functools.partial(fused, reps), out_shape=(jax.ShapeDtypeS...]
    all_gather x2 -> x0, waiting for transfers between devices: 38.5 us -> none  [the longest x1 38.5 us: on_device(): lax.all_gather(renewed.astype(jnp.bfloat16), 'rep', axis=1, tiled=True)]
    dot_general x2 -> x0, matrix products: 13.4 us -> none  [the longest x1 7.25 us: on_device(): jnp.dot(selected, lax.all_gather(weights, 'fsdp', axis=1, tiled=True)[0],...]
    broadcast_in_dim x1 -> x0, other arithmetic: 8.61 us -> none  [on_device(): return (values[None], merged[None], renewed, momentum)]
    unnamed x6 -> x8, local copies, waits for them, and re-layouts: 0.02 us -> 6.87 us
  transfers between devices with their start and end apart: 3 -> 0, of which waited for: 2 -> 0; matrix products, arithmetic and copies ran while one was open for 5% -> 0% of each run, Pallas kernels for 0% -> 0%
where the time goes in v1:
time: 81.6 us; the launch traced here: 81.1 us
  Pallas kernels  73.6 us (90%)
  local copies, waits for them, and re-layouts  6.87 us (8%)
    pallas_call x1, Pallas kernels, fused_call(): pl.pallas_call(functools.partial(fused, reps), out_shape=(jax.ShapeDtypeS...  73.6 us
    unnamed x8, local copies, waits for them, and re-layouts  6.87 us

profile of v1, /device:TPU:9, one launch (start us, length us, event | category | flops | bytes accessed | tf_op | source)
XLA Modules:
  0.0 81.1 jit_solution(4846413673753110129)
XLA Ops:
  0.6 73.6 %shard_map.102 = (bf16[1,256,1024]{2,1,0:T(8,128)(2,1)}, bf16[1,1152,1024]{2,1,0:T(8,128)(2,1)}, f32[1,144,1024]{2,1,0:T(8,128)}, f32[1,144,1024]{2,1,0:T(8,128)}) custom-call(bf16[1,256,4608]{2,1,0:T(8,128)(2,1)} %hidden.1, bf16[1,256,1024]{2,1,0:T(8,128)(2,1)} %upstream.1, bf16[1,1152,1024]{2,1,0:T(8,128)(2,1)} %weights.1, ...), custom_call_target="tpu_custom_call" | custom-call | flops 4831838208 | bytes 18874368 | tf_op jit(solution)/shard_map/pallas_call | solution.py:353
  74.2 1.9 %copy.15 = bf16[1,256,1024]{2,1,0:T(8,128)(2,1)} copy(bf16[1,256,1024]{2,1,0:T(8,128)(2,1)} %get-tuple-element.8) | data formatting | bytes 1048576
  76.1 0.0 copy-start.1
  76.1 0.0 copy-start
  76.1 3.4 %copy.16 = bf16[1,1152,1024]{2,1,0:T(8,128)(2,1)} copy(bf16[1,1152,1024]{2,1,0:T(8,128)(2,1)} %get-tuple-element.9) | data formatting | bytes 4718592
  79.5 0.0 copy-done.1
  79.5 0.8 %copy.17 = f32[1,144,1024]{2,1,0:T(8,128)} copy(f32[1,144,1024]{2,1,0:T(8,128)S(1)} %copy-done.1) | data formatting | bytes 1179648
  80.3 0.0 copy-done
  80.3 0.8 %copy.18 = f32[1,144,1024]{2,1,0:T(8,128)} copy(f32[1,144,1024]{2,1,0:T(8,128)S(1)} %copy-done) | data formatting | bytes 1179648
Async XLA Ops:
  76.1 3.4 %copy-start.1 = (f32[1,144,1024]{2,1,0:T(8,128)S(1)}, f32[1,144,1024]{2,1,0:T(8,128)}, u32[]{:S(2)}) copy-start(f32[1,144,1024]{2,1,0:T(8,128)} %get-tuple-element.10) | copy-start | bytes 1769476
  76.1 4.2 %copy-start = (f32[1,144,1024]{2,1,0:T(8,128)S(1)}, f32[1,144,1024]{2,1,0:T(8,128)}, u32[]{:S(2)}) copy-start(f32[1,144,1024]{2,1,0:T(8,128)} %get-tuple-element.11) | copy-start | bytes 1769476

commit v2 on v1

--- a/solution.py
+++ b/solution.py
@@ -21,7 +21,8 @@
 MESH = pl.DeviceIdType.MESH
 BF16 = jnp.bfloat16
 F32 = jnp.float32
-HALVES = 2
+CHUNKS = 4
+AHEAD = 4
 STRIP = 16
 
 
@@ -32,10 +33,10 @@
     return current - inner_rate * (stepped + decay_rate * current)
 
 
-def strips(rows, body):
-    @pl.loop(0, rows // STRIP)
+def strips(rows, body, tall=STRIP):
+    @pl.loop(0, rows // tall)
     def _(i):
-        body(pl.multiple_of(i * STRIP, STRIP))
+        body(pl.multiple_of(i * tall, STRIP))
 
 
 def fused(
@@ -53,7 +54,7 @@
     block, columns = weights.shape[1:]
     rows = block // reps
     layers = reps // 2
-    half = columns // HALVES
+    wide = columns // CHUNKS
     factor = float(width) ** (-0.5)
 
     me_rep = lax.axis_index("rep")
@@ -79,7 +80,7 @@
         return pl.ds(pl.multiple_of(owner * rows, STRIP), rows)
 
     def cols(h):
-        return pl.ds(h * half, half)
+        return pl.ds(h * wide, wide)
 
     def toks(j):
         return pl.ds(j * tokens, tokens)
@@ -132,12 +133,16 @@
         remote(dst, dst, u_send.at[j - 1], u_recv.at[j - 1], at_shard(shards[j])).wait_recv()
 
     order = tuple(range(1, layers)) + (0,)
+    pieces = [(h, d) for h in range(CHUNKS) for d in order]
+
+    def send_piece(h, d):
+        part = weights.at[0, row_block(layer(d) * 2 + (1 - x)), cols(h)]
+        go(remote(part, x_in.at[d, :, cols(h)], x_send.at[h, d], x_recv.at[h, d], at_rep(x_peer)))
+
+    for piece in pieces[:AHEAD]:
+        send_piece(*piece)
     send_hidden(3)
     send_hidden(2)
-    for h in range(HALVES):
-        for d in order:
-            part = weights.at[0, row_block(layer(d) * 2 + (1 - x)), cols(h)]
-            go(remote(part, x_in.at[d, :, cols(h)], x_send.at[h, d], x_recv.at[h, d], at_rep(x_peer)))
     send_hidden(1)
     send_upstream(1)
     send_upstream(2)
@@ -155,37 +160,39 @@
     project(1, p_out.at[0])
     go(remote(p_out.at[0], p_in.at[0], p_send.at[0], p_recv.at[0], at_shard(sibling)))
 
-    for h in range(HALVES):
+    tall = rows // 3 if rows % 48 == 0 else STRIP
+
+    def pairs(h):
         for d in order:
             dst = x_in.at[d, :, cols(h)]
             remote(dst, dst, x_send.at[h, d], x_recv.at[h, d], at_rep(x_peer)).wait_recv()
+            later = h * layers + order.index(d) + AHEAD
+            if later < len(pieces):
+                send_piece(*pieces[later])
             base = (layer(d) * 2 + x) * rows
 
-            def pair(i, d=d, h=h, base=base):
-                here = pl.ds(pl.multiple_of(base + i, STRIP), STRIP)
-                total = w[here, cols(h)].astype(F32) + x_in[d, pl.ds(i, STRIP), cols(h)].astype(F32)
+            def pair(i, d=d, base=base):
+                here = pl.ds(pl.multiple_of(base + i, STRIP), tall)
+                total = w[here, cols(h)].astype(F32) + x_in[d, pl.ds(i, tall), cols(h)].astype(F32)
                 if d == 0:
-                    acc[pl.ds(i, STRIP), cols(h)] = total
+                    acc[pl.ds(i, tall), cols(h)] = total
                 else:
-                    z_out[d - 1, pl.ds(i, STRIP), cols(h)] = total.astype(BF16)
-
-            strips(rows, pair)
+                    z_out[d - 1, pl.ds(i, tall), cols(h)] = total.astype(BF16)
+
+            strips(rows, pair, tall)
             if d:
                 go(remote(
                     z_out.at[d - 1, :, cols(h)], z_in.at[d - 1, :, cols(h)],
                     z_send.at[h, d - 1], z_recv.at[h, d - 1], at_rep(layer(d) * 2 + x),
                 ))
 
-    loads[3].wait()
-    loads[4].wait()
-    stores = []
-    for h in range(HALVES):
+    def renew(h):
         for d in range(1, layers):
             dst = z_in.at[d - 1, :, cols(h)]
             remote(dst, dst, z_send.at[h, d - 1], z_recv.at[h, d - 1], at_rep(me_rep)).wait_recv()
 
-        def outer(i, h=h):
-            here = pl.ds(i, STRIP)
+        def outer(i):
+            here = pl.ds(i, tall)
             summed = acc[here, cols(h)]
             for d in range(1, layers):
                 summed = summed + z_in[d - 1, here, cols(h)].astype(F32)
@@ -195,16 +202,39 @@
             renewed = now - outer_rate * (pseudo + outer_mu * momentum)
             mom[here, cols(h)] = momentum
             ren[here, cols(h)] = renewed
-            at = pl.ds(pl.multiple_of(me_rep * rows + i, STRIP), STRIP)
+            at = pl.ds(pl.multiple_of(me_rep * rows + i, STRIP), tall)
             spread[at, cols(h)] = renewed.astype(BF16)
 
-        strips(rows, outer)
+        strips(rows, outer, tall)
         own = spread.at[row_block(me_rep), cols(h)]
-        go(remote(own, own, gx_send.at[h, 0], gx_recv.at[h, 0], at_rep(x_peer)))
         for d in order[:-1]:
             go(remote(own, own, gz_send.at[h, d - 1], gz_recv.at[h, d - 1], at_rep(layer(d) * 2 + x)))
-    stores.append(pltpu.make_async_copy(ren, renewed_out.at[0], store_sem.at[0]))
-    stores.append(pltpu.make_async_copy(mom, momentum_out.at[0], store_sem.at[1]))
+        go(remote(own, own, gx_send.at[h, 0], gx_recv.at[h, 0], at_rep(x_peer)))
+
+    near_first = (1,) + tuple(range(layers - 1, 1, -1))
+
+    def forward(h):
+        for d in near_first:
+            part = spread.at[row_block(layer(-d) * 2 + x), cols(h)]
+            remote(part, part, gz_send.at[h, d - 1], gz_recv.at[h, d - 1], at_rep(me_rep)).wait_recv()
+            go(remote(part, part, gx_send.at[h, d], gx_recv.at[h, d], at_rep(x_peer)))
+
+    loads[3].wait()
+    loads[4].wait()
+    pairs(0)
+    pairs(1)
+    renew(0)
+    pairs(2)
+    renew(1)
+    forward(0)
+    pairs(3)
+    renew(2)
+    forward(1)
+    renew(3)
+    stores = [
+        pltpu.make_async_copy(ren, renewed_out.at[0], store_sem.at[0]),
+        pltpu.make_async_copy(mom, momentum_out.at[0], store_sem.at[1]),
+    ]
     stores[0].start()
     stores[1].start()
 
@@ -227,16 +257,9 @@
     strips(tokens, chip_sum)
     go(remote(y_out, y_in, p_send.at[2], p_recv.at[2], at_shard(across)))
 
-    def forward(h, d):
-        part = spread.at[row_block(layer(-d) * 2 + x), cols(h)]
-        remote(part, part, gz_send.at[h, d - 1], gz_recv.at[h, d - 1], at_rep(me_rep)).wait_recv()
-        go(remote(part, part, gx_send.at[h, d], gx_recv.at[h, d], at_rep(x_peer)))
-
     upstream_in(2)
     go(remote(u_all.at[toks(2)], u_all.at[toks(3)], u_send.at[2], u_recv.at[2], at_shard(sibling)))
-    near_first = (1,) + tuple(range(layers - 1, 1, -1))
-    for d in near_first:
-        forward(0, d)
+    forward(2)
     loads[2].wait()
     loads[5].wait()
     loads[6].wait()
@@ -266,8 +289,7 @@
         strips(part_rows, step)
 
     inner(0)
-    for d in near_first:
-        forward(1, d)
+    forward(3)
     inner(1)
     inner(2)
 
@@ -302,7 +324,7 @@
         merge(layer(-d) * 2 + x, i + 1)
     for i, d in enumerate((0,) + near_first):
         owner = layer(-d) * 2 + (1 - x)
-        for h in range(HALVES):
+        for h in range(CHUNKS):
             part = spread.at[row_block(owner), cols(h)]
             remote(part, part, gx_send.at[h, d], gx_recv.at[h, d], at_rep(x_peer)).wait_recv()
         merge(owner, layers + i)
@@ -344,10 +366,10 @@
         pltpu.VMEM((rows, columns), F32),
         dma((7,)), dma((3,)), dma((reps,)),
         dma((3,)), dma((3,)), dma((3,)), dma((3,)), dma((3,)), dma((3,)),
-        dma((HALVES, layers)), dma((HALVES, layers)),
-        dma((HALVES, layers - 1)), dma((HALVES, layers - 1)),
-        dma((HALVES, layers - 1)), dma((HALVES, layers - 1)),
-        dma((HALVES, layers)), dma((HALVES, layers)),
+        dma((CHUNKS, layers)), dma((CHUNKS, layers)),
+        dma((CHUNKS, layers - 1)), dma((CHUNKS, layers - 1)),
+        dma((CHUNKS, layers - 1)), dma((CHUNKS, layers - 1)),
+        dma((CHUNKS, layers)), dma((CHUNKS, layers)),
     ]
     anywhere = pl.BlockSpec(memory_space=pl.ANY)
     return pl.pallas_call(

time: 81.6 us -> 79.4 us (0.973)
  Pallas kernels: 73.6 us -> 70.8 us
    pallas_call x1, Pallas kernels: 73.6 us -> 70.8 us  [fused_call(): pl.pallas_call(functools.partial(fused, reps), out_shape=(jax.ShapeDtypeS...]
where the time goes in v2:
time: 79.4 us; the launch traced here: 78.3 us
  Pallas kernels  70.8 us (89%)
  local copies, waits for them, and re-layouts  6.87 us (9%)
    pallas_call x1, Pallas kernels, fused_call(): pl.pallas_call(functools.partial(fused, reps), out_shape=(jax.ShapeDtypeS...  70.8 us
    unnamed x8, local copies, waits for them, and re-layouts  6.87 us

profile of v2, /device:TPU:9, one launch (start us, length us, event | category | flops | bytes accessed | tf_op | source)
XLA Modules:
  0.0 78.3 jit_solution(8106084599109527454)
XLA Ops:
  0.6 70.8 %shard_map.102 = (bf16[1,256,1024]{2,1,0:T(8,128)(2,1)}, bf16[1,1152,1024]{2,1,0:T(8,128)(2,1)}, f32[1,144,1024]{2,1,0:T(8,128)}, f32[1,144,1024]{2,1,0:T(8,128)}) custom-call(bf16[1,256,4608]{2,1,0:T(8,128)(2,1)} %hidden.1, bf16[1,256,1024]{2,1,0:T(8,128)(2,1)} %upstream.1, bf16[1,1152,1024]{2,1,0:T(8,128)(2,1)} %weights.1, ...), custom_call_target="tpu_custom_call" | custom-call | flops 4831838208 | bytes 18874368 | tf_op jit(solution)/shard_map/pallas_call | solution.py:375
  71.4 1.9 %copy.15 = bf16[1,256,1024]{2,1,0:T(8,128)(2,1)} copy(bf16[1,256,1024]{2,1,0:T(8,128)(2,1)} %get-tuple-element.8) | data formatting | bytes 1048576
  73.3 0.0 copy-start.1
  73.3 0.0 copy-start
  73.3 3.4 %copy.16 = bf16[1,1152,1024]{2,1,0:T(8,128)(2,1)} copy(bf16[1,1152,1024]{2,1,0:T(8,128)(2,1)} %get-tuple-element.9) | data formatting | bytes 4718592
  76.7 0.0 copy-done.1
  76.7 0.8 %copy.17 = f32[1,144,1024]{2,1,0:T(8,128)} copy(f32[1,144,1024]{2,1,0:T(8,128)S(1)} %copy-done.1) | data formatting | bytes 1179648
  77.5 0.0 copy-done
  77.5 0.8 %copy.18 = f32[1,144,1024]{2,1,0:T(8,128)} copy(f32[1,144,1024]{2,1,0:T(8,128)S(1)} %copy-done) | data formatting | bytes 1179648
Async XLA Ops:
  73.3 3.4 %copy-start.1 = (f32[1,144,1024]{2,1,0:T(8,128)S(1)}, f32[1,144,1024]{2,1,0:T(8,128)}, u32[]{:S(2)}) copy-start(f32[1,144,1024]{2,1,0:T(8,128)} %get-tuple-element.10) | copy-start | bytes 1769476
  73.3 4.2 %copy-start = (f32[1,144,1024]{2,1,0:T(8,128)S(1)}, f32[1,144,1024]{2,1,0:T(8,128)}, u32[]{:S(2)}) copy-start(f32[1,144,1024]{2,1,0:T(8,128)} %get-tuple-element.11) | copy-start | bytes 1769476

commit v3 on v2

--- a/solution.py
+++ b/solution.py
@@ -33,6 +33,13 @@
     return current - inner_rate * (stepped + decay_rate * current)
 
 
+def half_inner(raw, first, second, current, factor):
+    scale = mixing * inner_rate / bias_one
+    moment = (scale * beta_one) * first + (scale * (1.0 - beta_one) * factor) * raw
+    second_new = (beta_two / bias_two) * second + ((1.0 - beta_two) * factor * factor / bias_two) * (raw * raw)
+    return (mixing * (1.0 - inner_rate * decay_rate)) * current - moment / (jnp.sqrt(second_new) + epsilon)
+
+
 def strips(rows, body, tall=STRIP):
     @pl.loop(0, rows // tall)
     def _(i):
@@ -43,8 +50,8 @@
     reps,
     hidden, upstream, weights, moment_one, moment_two, global_params, outer_momentum,
     values_out, merged_out, renewed_out, momentum_out,
-    h_all, u_all, w, m1, m2, g, om,
-    x_in, z_out, z_in, acc, spread, grad, p_own, p_out, p_in, y_out, y_in,
+    h_all, h_t, u_all, w, m1, m2, g, om,
+    x_in, z_out, z_in, acc, spread, grad, p_own, p_far, p_out, p_in, y_out, y_in,
     val, mer, ren, mom,
     local_sem, store_sem, merged_sem,
     h_send, h_recv, u_send, u_recv, p_send, p_recv,
@@ -125,12 +132,22 @@
         dst = h_all.at[toks(j)]
         remote(dst, dst, h_send.at[j - 1], h_recv.at[j - 1], at_shard(shards[j])).wait_recv()
 
-    def send_upstream(j):
-        go(remote(upstream.at[0], u_all.at[toks(j)], u_send.at[j - 1], u_recv.at[j - 1], at_shard(shards[j])))
-
-    def upstream_in(j):
-        dst = u_all.at[toks(j)]
-        remote(dst, dst, u_send.at[j - 1], u_recv.at[j - 1], at_shard(shards[j])).wait_recv()
+    def send_upstream(j, h):
+        go(remote(
+            upstream.at[0, :, cols(h)], u_all.at[toks(j), cols(h)],
+            u_send.at[j - 1, h], u_recv.at[j - 1, h], at_shard(shards[j]),
+        ))
+
+    def upstream_in(j, h):
+        dst = u_all.at[toks(j), cols(h)]
+        remote(dst, dst, u_send.at[j - 1, h], u_recv.at[j - 1, h], at_shard(shards[j])).wait_recv()
+
+    def pass_upstream(h):
+        upstream_in(2, h)
+        go(remote(
+            u_all.at[toks(2), cols(h)], u_all.at[toks(3), cols(h)],
+            u_send.at[2, h], u_recv.at[2, h], at_shard(sibling),
+        ))
 
     order = tuple(range(1, layers)) + (0,)
     pieces = [(h, d) for h in range(CHUNKS) for d in order]
@@ -144,8 +161,8 @@
     send_hidden(3)
     send_hidden(2)
     send_hidden(1)
-    send_upstream(1)
-    send_upstream(2)
+    for h in range(CHUNKS):
+        send_upstream(1, h)
 
     def project(j, dst):
         @pl.loop(0, columns // 256)
@@ -153,12 +170,20 @@
             at = pl.ds(pl.multiple_of(n * 256, 256), 256)
             dst[:, at] = jnp.dot(h_all[toks(j), :], w[:, at], preferred_element_type=F32)
 
+    def turn(j):
+        @pl.loop(0, block // 128)
+        def _(i):
+            at = pl.ds(pl.multiple_of(i * 128, 128), 128)
+            h_t[at, toks(j)] = h_all[toks(j), at].T
+
     loads[0].wait()
     loads[1].wait()
     project(0, p_own)
+    turn(0)
     hidden_in(1)
     project(1, p_out.at[0])
     go(remote(p_out.at[0], p_in.at[0], p_send.at[0], p_recv.at[0], at_shard(sibling)))
+    turn(1)
 
     tall = rows // 3 if rows % 48 == 0 else STRIP
 
@@ -219,16 +244,54 @@
             remote(part, part, gz_send.at[h, d - 1], gz_recv.at[h, d - 1], at_rep(me_rep)).wait_recv()
             go(remote(part, part, gx_send.at[h, d], gx_recv.at[h, d], at_rep(x_peer)))
 
+    part_rows = block // 3
+    high = 48 if block % 48 == 0 else STRIP
+
+    def inner(h):
+        upstream_in(1, h)
+        upstream_in(3, h)
+
+        @pl.loop(0, 3)
+        def _(part):
+            at = pl.ds(pl.multiple_of(part * part_rows, STRIP), part_rows)
+            grad[at, cols(h)] = jnp.dot(h_t[at, :], u_all[:, cols(h)], preferred_element_type=F32)
+
+        def step(i):
+            here = (pl.ds(i, high), cols(h))
+            grad[here] = half_inner(
+                grad[here], m1[here].astype(F32), m2[here].astype(F32), w[here].astype(F32), factor
+            )
+
+        strips(block, step, high)
+
     loads[3].wait()
     loads[4].wait()
     pairs(0)
     pairs(1)
     renew(0)
+    send_upstream(2, 0)
     pairs(2)
     renew(1)
+    send_upstream(2, 1)
     forward(0)
     pairs(3)
+
+    hidden_in(3)
+    send_upstream(2, 2)
+    send_upstream(2, 3)
+    project(3, p_out.at[1])
+    go(remote(p_out.at[1], p_in.at[1], p_send.at[1], p_recv.at[1], at_shard(sibling)))
     renew(2)
+    hidden_in(2)
+    project(2, p_far)
+    remote(p_in.at[1], p_in.at[1], p_send.at[1], p_recv.at[1], at_shard(sibling)).wait_recv()
+
+    def chip_sum(i):
+        here = pl.ds(i, STRIP)
+        y_out[here, :] = (p_far[here, :] + p_in[1, here, :]).astype(BF16)
+
+    strips(tokens, chip_sum)
+    go(remote(y_out, y_in, p_send.at[2], p_recv.at[2], at_shard(across)))
     forward(1)
     renew(3)
     stores = [
@@ -237,61 +300,21 @@
     ]
     stores[0].start()
     stores[1].start()
-
-    hidden_in(3)
-    project(3, p_out.at[1])
-    go(remote(p_out.at[1], p_in.at[1], p_send.at[1], p_recv.at[1], at_shard(sibling)))
-    hidden_in(2)
-
-    @pl.loop(0, columns // 256)
-    def _(n):
-        at = pl.ds(pl.multiple_of(n * 256, 256), 256)
-        grad[pl.ds(0, tokens), at] = jnp.dot(h_all[toks(2), :], w[:, at], preferred_element_type=F32)
-
-    remote(p_in.at[1], p_in.at[1], p_send.at[1], p_recv.at[1], at_shard(sibling)).wait_recv()
-
-    def chip_sum(i):
-        here = pl.ds(i, STRIP)
-        y_out[here, :] = (grad[here, :] + p_in[1, here, :]).astype(BF16)
-
-    strips(tokens, chip_sum)
-    go(remote(y_out, y_in, p_send.at[2], p_recv.at[2], at_shard(across)))
-
-    upstream_in(2)
-    go(remote(u_all.at[toks(2)], u_all.at[toks(3)], u_send.at[2], u_recv.at[2], at_shard(sibling)))
-    forward(2)
+    turn(3)
+    turn(2)
     loads[2].wait()
     loads[5].wait()
     loads[6].wait()
-    upstream_in(1)
-    upstream_in(3)
-
-    part_rows = block // 3
-
-    def inner(part):
-        lhs = h_all[:, pl.ds(part * part_rows, part_rows)]
-        base = part * part_rows
-
-        @pl.loop(0, columns // 256)
-        def _(n):
-            at = pl.ds(pl.multiple_of(n * 256, 256), 256)
-            grad[pl.ds(base, part_rows), at] = lax.dot_general(
-                lhs, u_all[:, at], (((0,), (0,)), ((), ())), preferred_element_type=F32
-            )
-
-        def step(i):
-            here = pl.ds(pl.multiple_of(base + i, STRIP), STRIP)
-            updated = inner_step(
-                grad[here, :] * factor, m1[here, :].astype(F32), m2[here, :].astype(F32), w[here, :].astype(F32)
-            )
-            grad[here, :] = mixing * updated
-
-        strips(part_rows, step)
-
+    pass_upstream(0)
+    pass_upstream(1)
     inner(0)
+    forward(2)
+    pass_upstream(2)
+    inner(1)
+    pass_upstream(3)
     forward(3)
-    inner(1)
     inner(2)
+    inner(3)
 
     remote(p_in.at[0], p_in.at[0], p_send.at[0], p_recv.at[0], at_shard(sibling)).wait_recv()
     remote(y_in, y_in, p_send.at[2], p_recv.at[2], at_shard(across)).wait_recv()
@@ -343,6 +366,7 @@
     dma = pltpu.SemaphoreType.DMA
     scratch = [
         pltpu.VMEM((4 * tokens, block), BF16),
+        pltpu.VMEM((block, 4 * tokens), BF16),
         pltpu.VMEM((4 * tokens, columns), BF16),
         pltpu.VMEM((block, columns), BF16),
         pltpu.VMEM((block, columns), BF16),
@@ -356,6 +380,7 @@
         pltpu.VMEM((block, columns), BF16),
         pltpu.VMEM((block, columns), F32),
         pltpu.VMEM((tokens, columns), F32),
+        pltpu.VMEM((tokens, columns), F32),
         pltpu.VMEM((2, tokens, columns), F32),
         pltpu.VMEM((2, tokens, columns), F32),
         pltpu.VMEM((tokens, columns), BF16),
@@ -365,7 +390,7 @@
         pltpu.VMEM((rows, columns), F32),
         pltpu.VMEM((rows, columns), F32),
         dma((7,)), dma((3,)), dma((reps,)),
-        dma((3,)), dma((3,)), dma((3,)), dma((3,)), dma((3,)), dma((3,)),
+        dma((3,)), dma((3,)), dma((3, CHUNKS)), dma((3, CHUNKS)), dma((3,)), dma((3,)),
         dma((CHUNKS, layers)), dma((CHUNKS, layers)),
         dma((CHUNKS, layers - 1)), dma((CHUNKS, layers - 1)),
         dma((CHUNKS, layers - 1)), dma((CHUNKS, layers - 1)),

time: 79.4 us -> 79.1 us (level)
  the two profiles are of different devices: /device:TPU:9 before, /device:TPU:29 now
where the time goes in v3:
time: 79.1 us; the launch traced here: 79 us
  Pallas kernels  71.5 us (90%)
  local copies, waits for them, and re-layouts  6.87 us (9%)
    pallas_call x1, Pallas kernels, fused_call(): pl.pallas_call(functools.partial(fused, reps), out_shape=(jax.ShapeDtypeS...  71.5 us
    unnamed x8, local copies, waits for them, and re-layouts  6.87 us

profile of v3, /device:TPU:29, one launch (start us, length us, event | category | flops | bytes accessed | tf_op | source)
XLA Modules:
  0.0 79.0 jit_solution(8774006675195990239)
XLA Ops:
  0.6 71.5 %shard_map.102 = (bf16[1,256,1024]{2,1,0:T(8,128)(2,1)}, bf16[1,1152,1024]{2,1,0:T(8,128)(2,1)}, f32[1,144,1024]{2,1,0:T(8,128)}, f32[1,144,1024]{2,1,0:T(8,128)}) custom-call(bf16[1,256,4608]{2,1,0:T(8,128)(2,1)} %hidden.1, bf16[1,256,1024]{2,1,0:T(8,128)(2,1)} %upstream.1, bf16[1,1152,1024]{2,1,0:T(8,128)(2,1)} %weights.1, ...), custom_call_target="tpu_custom_call" | custom-call | flops 4831838208 | bytes 18874368 | tf_op jit(solution)/shard_map/pallas_call | solution.py:400
  72.1 1.9 %copy.15 = bf16[1,256,1024]{2,1,0:T(8,128)(2,1)} copy(bf16[1,256,1024]{2,1,0:T(8,128)(2,1)} %get-tuple-element.8) | data formatting | bytes 1048576
  74.0 0.0 copy-start.1
  74.0 0.0 copy-start
  74.0 3.4 %copy.16 = bf16[1,1152,1024]{2,1,0:T(8,128)(2,1)} copy(bf16[1,1152,1024]{2,1,0:T(8,128)(2,1)} %get-tuple-element.9) | data formatting | bytes 4718592
  77.3 0.0 copy-done.1
  77.4 0.8 %copy.17 = f32[1,144,1024]{2,1,0:T(8,128)} copy(f32[1,144,1024]{2,1,0:T(8,128)S(1)} %copy-done.1) | data formatting | bytes 1179648
  78.2 0.0 copy-done
  78.2 0.8 %copy.18 = f32[1,144,1024]{2,1,0:T(8,128)} copy(f32[1,144,1024]{2,1,0:T(8,128)S(1)} %copy-done) | data formatting | bytes 1179648
Async XLA Ops:
  74.0 3.4 %copy-start.1 = (f32[1,144,1024]{2,1,0:T(8,128)S(1)}, f32[1,144,1024]{2,1,0:T(8,128)}, u32[]{:S(2)}) copy-start(f32[1,144,1024]{2,1,0:T(8,128)} %get-tuple-element.10) | copy-start | bytes 1769476
  74.0 4.2 %copy-start = (f32[1,144,1024]{2,1,0:T(8,128)S(1)}, f32[1,144,1024]{2,1,0:T(8,128)}, u32[]{:S(2)}) copy-start(f32[1,144,1024]{2,1,0:T(8,128)} %get-tuple-element.11) | copy-start | bytes 1769476

commit v4 on v3

--- a/solution.py
+++ b/solution.py
@@ -22,7 +22,7 @@
 BF16 = jnp.bfloat16
 F32 = jnp.float32
 CHUNKS = 4
-AHEAD = 4
+AHEAD = 8
 STRIP = 16
 
 
@@ -49,11 +49,10 @@
 def fused(
     reps,
     hidden, upstream, weights, moment_one, moment_two, global_params, outer_momentum,
-    values_out, merged_out, renewed_out, momentum_out,
+    val, mer, ren, mom,
     h_all, h_t, u_all, w, m1, m2, g, om,
     x_in, z_out, z_in, acc, spread, grad, p_own, p_far, p_out, p_in, y_out, y_in,
-    val, mer, ren, mom,
-    local_sem, store_sem, merged_sem,
+    local_sem,
     h_send, h_recv, u_send, u_recv, p_send, p_recv,
     x_send, x_recv, z_send, z_recv, gz_send, gz_recv, gx_send, gx_recv,
 ):
@@ -273,15 +272,17 @@
     pairs(2)
     renew(1)
     send_upstream(2, 1)
+    pairs(3)
+    renew(2)
     forward(0)
-    pairs(3)
-
-    hidden_in(3)
     send_upstream(2, 2)
     send_upstream(2, 3)
+    renew(3)
+    forward(1)
+
+    hidden_in(3)
     project(3, p_out.at[1])
     go(remote(p_out.at[1], p_in.at[1], p_send.at[1], p_recv.at[1], at_shard(sibling)))
-    renew(2)
     hidden_in(2)
     project(2, p_far)
     remote(p_in.at[1], p_in.at[1], p_send.at[1], p_recv.at[1], at_shard(sibling)).wait_recv()
@@ -292,14 +293,7 @@
 
     strips(tokens, chip_sum)
     go(remote(y_out, y_in, p_send.at[2], p_recv.at[2], at_shard(across)))
-    forward(1)
-    renew(3)
-    stores = [
-        pltpu.make_async_copy(ren, renewed_out.at[0], store_sem.at[0]),
-        pltpu.make_async_copy(mom, momentum_out.at[0], store_sem.at[1]),
-    ]
-    stores[0].start()
-    stores[1].start()
+    forward(2)
     turn(3)
     turn(2)
     loads[2].wait()
@@ -308,11 +302,10 @@
     pass_upstream(0)
     pass_upstream(1)
     inner(0)
-    forward(2)
+    forward(3)
     pass_upstream(2)
     inner(1)
     pass_upstream(3)
-    forward(3)
     inner(2)
     inner(3)
 
@@ -325,10 +318,8 @@
         val[here, :] = (total * factor).astype(BF16)
 
     strips(tokens, finish)
-    stores.append(pltpu.make_async_copy(val, values_out.at[0], store_sem.at[2]))
-    stores[2].start()
-
-    def merge(owner, slot):
+
+    def merge(owner):
         base = owner * rows
 
         def body(i):
@@ -336,26 +327,19 @@
             mer[here, :] = (grad[here, :] + (1.0 - mixing) * spread[here, :].astype(F32)).astype(BF16)
 
         strips(rows, body)
-        copy = pltpu.make_async_copy(
-            mer.at[row_block(owner)], merged_out.at[0, row_block(owner)], merged_sem.at[slot]
-        )
-        copy.start()
-        stores.append(copy)
-
-    merge(me_rep, 0)
-    for i, d in enumerate(near_first):
-        merge(layer(-d) * 2 + x, i + 1)
-    for i, d in enumerate((0,) + near_first):
+
+    merge(me_rep)
+    for d in near_first:
+        merge(layer(-d) * 2 + x)
+    for d in (0,) + near_first:
         owner = layer(-d) * 2 + (1 - x)
         for h in range(CHUNKS):
             part = spread.at[row_block(owner), cols(h)]
             remote(part, part, gx_send.at[h, d], gx_recv.at[h, d], at_rep(x_peer)).wait_recv()
-        merge(owner, layers + i)
+        merge(owner)
 
     for copy in sent:
         copy.wait_send()
-    for copy in stores:
-        copy.wait()
 
 
 def fused_call(reps, hidden, upstream, weights, moment_one, moment_two, global_params, outer_momentum):
@@ -385,11 +369,7 @@
         pltpu.VMEM((2, tokens, columns), F32),
         pltpu.VMEM((tokens, columns), BF16),
         pltpu.VMEM((tokens, columns), BF16),
-        pltpu.VMEM((tokens, columns), BF16),
-        pltpu.VMEM((block, columns), BF16),
-        pltpu.VMEM((rows, columns), F32),
-        pltpu.VMEM((rows, columns), F32),
-        dma((7,)), dma((3,)), dma((reps,)),
+        dma((7,)),
         dma((3,)), dma((3,)), dma((3, CHUNKS)), dma((3, CHUNKS)), dma((3,)), dma((3,)),
         dma((CHUNKS, layers)), dma((CHUNKS, layers)),
         dma((CHUNKS, layers - 1)), dma((CHUNKS, layers - 1)),
@@ -397,24 +377,44 @@
         dma((CHUNKS, layers)), dma((CHUNKS, layers)),
     ]
     anywhere = pl.BlockSpec(memory_space=pl.ANY)
-    return pl.pallas_call(
+    results = pl.pallas_call(
         functools.partial(fused, reps),
         out_shape=(
-            jax.ShapeDtypeStruct((1, tokens, columns), BF16),
-            jax.ShapeDtypeStruct(weights.shape, BF16),
-            jax.ShapeDtypeStruct(global_params.shape, F32),
-            jax.ShapeDtypeStruct(global_params.shape, F32),
+            pltpu.VMEM((tokens, columns), BF16),
+            pltpu.VMEM((block, columns), BF16),
+            pltpu.VMEM((rows, columns), F32),
+            pltpu.VMEM((rows, columns), F32),
         ),
         in_specs=[anywhere] * 7,
-        out_specs=[anywhere] * 4,
+        out_specs=[pl.BlockSpec(memory_space=pltpu.VMEM)] * 4,
         scratch_shapes=scratch,
         compiler_params=pltpu.CompilerParams(
-            collective_id=0, has_side_effects=True, vmem_limit_bytes=56 * 1024 * 1024
+            collective_id=0, has_side_effects=True, vmem_limit_bytes=59 * 1024 * 1024
         ),
         cost_estimate=pl.CostEstimate(
             flops=4 * tokens * hidden.shape[2] * columns, bytes_accessed=18 * 1024 * 1024, transcendentals=0
         ),
     )(hidden, upstream, weights, moment_one, moment_two, global_params, outer_momentum)
+    return pl.pallas_call(
+        write_out,
+        out_shape=tuple(jax.ShapeDtypeStruct((1,) + a.shape, a.dtype) for a in results),
+        in_specs=[pl.BlockSpec(memory_space=pltpu.VMEM)] * 4,
+        out_specs=[anywhere] * 4,
+        scratch_shapes=[dma((4,))],
+        compiler_params=pltpu.CompilerParams(vmem_limit_bytes=8 * 1024 * 1024),
+        cost_estimate=pl.CostEstimate(flops=0, bytes_accessed=8 * 1024 * 1024, transcendentals=0),
+    )(*results)
+
+
+def write_out(*refs):
+    sources, targets, done = refs[:4], refs[4:8], refs[8]
+    copies = [
+        pltpu.make_async_copy(a, b.at[0], done.at[i]) for i, (a, b) in enumerate(zip(sources, targets))
+    ]
+    for copy in copies:
+        copy.start()
+    for copy in copies:
+        copy.wait()
 
 
 def collective_form(hidden, upstream, weights, moment_one, moment_two, global_params, outer_momentum):

time: 79.1 us -> 74.8 us (0.946)
  the two profiles are of different devices: /device:TPU:29 before, /device:TPU:9 now
where the time goes in v4:
time: 74.8 us; the launch traced here: 74.6 us
  Pallas kernels  74 us (99%)
    pallas_call x1, Pallas kernels, fused_call(): pl.pallas_call(functools.partial(fused, reps), out_shape=(pltpu.VMEM((tok...  72 us
    pallas_call x1, Pallas kernels, fused_call(): pl.pallas_call(write_out, out_shape=tuple((jax.ShapeDtypeStruct((1,) + a....  2 us

profile of v4, /device:TPU:9, one launch (start us, length us, event | category | flops | bytes accessed | tf_op | source)
XLA Modules:
  0.0 74.6 jit_solution(11547777015351722540)
XLA Ops:
  0.6 72.0 %shard_map.102 = (bf16[256,1024]{1,0:T(8,128)(2,1)S(1)}, bf16[1152,1024]{1,0:T(8,128)(2,1)S(1)}, f32[144,1024]{1,0:T(8,128)S(1)}, f32[144,1024]{1,0:T(8,128)S(1)}) custom-call(bf16[1,256,4608]{2,1,0:T(8,128)(2,1)} %hidden.1, bf16[1,256,1024]{2,1,0:T(8,128)(2,1)} %upstream.1, bf16[1,1152,1024]{2,1,0:T(8,128)(2,1)} %weights.1, ...), custom_call_target="tpu_custom_call" | custom-call | flops 4831838208 | bytes 18874368 | tf_op jit(solution)/shard_map/pallas_call | solution.py:380
  72.6 2.0 %shard_map.103 = (bf16[1,256,1024]{2,1,0:T(8,128)(2,1)}, bf16[1,1152,1024]{2,1,0:T(8,128)(2,1)}, f32[1,144,1024]{2,1,0:T(8,128)}, f32[1,144,1024]{2,1,0:T(8,128)}) custom-call(bf16[256,1024]{1,0:T(8,128)(2,1)S(1)} %get-tuple-element.8.refs_0_, bf16[1152,1024]{1,0:T(8,128)(2,1)S(1)} %get-tuple-element.9.refs_1_, f32[144,1024]{1,0:T(8,128)S(1)} %get-tuple-element.10.refs_2_, ...), custom_call_target="tpu_custom_call" | custom-call | bytes 8388608 | tf_op jit(solution)/shard_map/pallas_call | solution.py:398

commit v5 on v4

--- a/solution.py
+++ b/solution.py
@@ -21,7 +21,8 @@
 MESH = pl.DeviceIdType.MESH
 BF16 = jnp.bfloat16
 F32 = jnp.float32
-CHUNKS = 4
+CHUNKS = 3
+UP_CHUNKS = 2
 AHEAD = 8
 STRIP = 16
 
@@ -60,7 +61,8 @@
     block, columns = weights.shape[1:]
     rows = block // reps
     layers = reps // 2
-    wide = columns // CHUNKS
+    wide = columns // UP_CHUNKS
+    short = rows // CHUNKS
     factor = float(width) ** (-0.5)
 
     me_rep = lax.axis_index("rep")
@@ -82,8 +84,11 @@
     def at_rep(r):
         return (r, me_shard)
 
-    def row_block(owner):
-        return pl.ds(pl.multiple_of(owner * rows, STRIP), rows)
+    def piece_of(owner, h):
+        return pl.ds(pl.multiple_of(owner * rows + h * short, STRIP), short)
+
+    def sub(h):
+        return pl.ds(h * short, short)
 
     def cols(h):
         return pl.ds(h * wide, wide)
@@ -152,15 +157,15 @@
     pieces = [(h, d) for h in range(CHUNKS) for d in order]
 
     def send_piece(h, d):
-        part = weights.at[0, row_block(layer(d) * 2 + (1 - x)), cols(h)]
-        go(remote(part, x_in.at[d, :, cols(h)], x_send.at[h, d], x_recv.at[h, d], at_rep(x_peer)))
+        part = weights.at[0, piece_of(layer(d) * 2 + (1 - x), h)]
+        go(remote(part, x_in.at[d, sub(h)], x_send.at[h, d], x_recv.at[h, d], at_rep(x_peer)))
 
     for piece in pieces[:AHEAD]:
         send_piece(*piece)
     send_hidden(3)
     send_hidden(2)
     send_hidden(1)
-    for h in range(CHUNKS):
+    for h in range(UP_CHUNKS):
         send_upstream(1, h)
 
     def project(j, dst):
@@ -184,53 +189,52 @@
     go(remote(p_out.at[0], p_in.at[0], p_send.at[0], p_recv.at[0], at_shard(sibling)))
     turn(1)
 
-    tall = rows // 3 if rows % 48 == 0 else STRIP
-
     def pairs(h):
         for d in order:
-            dst = x_in.at[d, :, cols(h)]
+            dst = x_in.at[d, sub(h)]
             remote(dst, dst, x_send.at[h, d], x_recv.at[h, d], at_rep(x_peer)).wait_recv()
             later = h * layers + order.index(d) + AHEAD
             if later < len(pieces):
                 send_piece(*pieces[later])
-            base = (layer(d) * 2 + x) * rows
+            base = (layer(d) * 2 + x) * rows + h * short
 
             def pair(i, d=d, base=base):
-                here = pl.ds(pl.multiple_of(base + i, STRIP), tall)
-                total = w[here, cols(h)].astype(F32) + x_in[d, pl.ds(i, tall), cols(h)].astype(F32)
+                here = pl.ds(pl.multiple_of(base + i, STRIP), STRIP)
+                mine = pl.ds(pl.multiple_of(h * short + i, STRIP), STRIP)
+                total = w[here, :].astype(F32) + x_in[d, mine, :].astype(F32)
                 if d == 0:
-                    acc[pl.ds(i, tall), cols(h)] = total
+                    acc[mine, :] = total
                 else:
-                    z_out[d - 1, pl.ds(i, tall), cols(h)] = total.astype(BF16)
-
-            strips(rows, pair, tall)
+                    z_out[d - 1, mine, :] = total.astype(BF16)
+
+            strips(short, pair)
             if d:
                 go(remote(
-                    z_out.at[d - 1, :, cols(h)], z_in.at[d - 1, :, cols(h)],
+                    z_out.at[d - 1, sub(h)], z_in.at[d - 1, sub(h)],
                     z_send.at[h, d - 1], z_recv.at[h, d - 1], at_rep(layer(d) * 2 + x),
                 ))
 
     def renew(h):
         for d in range(1, layers):
-            dst = z_in.at[d - 1, :, cols(h)]
+            dst = z_in.at[d - 1, sub(h)]
             remote(dst, dst, z_send.at[h, d - 1], z_recv.at[h, d - 1], at_rep(me_rep)).wait_recv()
 
         def outer(i):
-            here = pl.ds(i, tall)
-            summed = acc[here, cols(h)]
+            here = pl.ds(pl.multiple_of(h * short + i, STRIP), STRIP)
+            summed = acc[here, :]
             for d in range(1, layers):
-                summed = summed + z_in[d - 1, here, cols(h)].astype(F32)
-            now = g[here, cols(h)]
+                summed = summed + z_in[d - 1, here, :].astype(F32)
+            now = g[here, :]
             pseudo = now - summed / reps
-            momentum = outer_mu * om[here, cols(h)] + pseudo
+            momentum = outer_mu * om[here, :] + pseudo
             renewed = now - outer_rate * (pseudo + outer_mu * momentum)
-            mom[here, cols(h)] = momentum
-            ren[here, cols(h)] = renewed
-            at = pl.ds(pl.multiple_of(me_rep * rows + i, STRIP), tall)
-            spread[at, cols(h)] = renewed.astype(BF16)
-
-        strips(rows, outer, tall)
-        own = spread.at[row_block(me_rep), cols(h)]
+            mom[here, :] = momentum
+            ren[here, :] = renewed
+            at = pl.ds(pl.multiple_of(me_rep * rows + h * short + i, STRIP), STRIP)
+            spread[at, :] = renewed.astype(BF16)
+
+        strips(short, outer)
+        own = spread.at[piece_of(me_rep, h)]
         for d in order[:-1]:
             go(remote(own, own, gz_send.at[h, d - 1], gz_recv.at[h, d - 1], at_rep(layer(d) * 2 + x)))
         go(remote(own, own, gx_send.at[h, 0], gx_recv.at[h, 0], at_rep(x_peer)))
@@ -239,12 +243,12 @@
 
     def forward(h):
         for d in near_first:
-            part = spread.at[row_block(layer(-d) * 2 + x), cols(h)]
+            part = spread.at[piece_of(layer(-d) * 2 + x, h)]
             remote(part, part, gz_send.at[h, d - 1], gz_recv.at[h, d - 1], at_rep(me_rep)).wait_recv()
             go(remote(part, part, gx_send.at[h, d], gx_recv.at[h, d], at_rep(x_peer)))
 
     part_rows = block // 3
-    high = 48 if block % 48 == 0 else STRIP
+    high = STRIP
 
     def inner(h):
         upstream_in(1, h)
@@ -271,13 +275,9 @@
     send_upstream(2, 0)
     pairs(2)
     renew(1)
+    forward(0)
     send_upstream(2, 1)
-    pairs(3)
     renew(2)
-    forward(0)
-    send_upstream(2, 2)
-    send_upstream(2, 3)
-    renew(3)
     forward(1)
 
     hidden_in(3)
@@ -302,12 +302,7 @@
     pass_upstream(0)
     pass_upstream(1)
     inner(0)
-    forward(3)
-    pass_upstream(2)
     inner(1)
-    pass_upstream(3)
-    inner(2)
-    inner(3)
 
     remote(p_in.at[0], p_in.at[0], p_send.at[0], p_recv.at[0], at_shard(sibling)).wait_recv()
     remote(y_in, y_in, p_send.at[2], p_recv.at[2], at_shard(across)).wait_recv()
@@ -334,7 +329,7 @@
     for d in (0,) + near_first:
         owner = layer(-d) * 2 + (1 - x)
         for h in range(CHUNKS):
-            part = spread.at[row_block(owner), cols(h)]
+            part = spread.at[piece_of(owner, h)]
             remote(part, part, gx_send.at[h, d], gx_recv.at[h, d], at_rep(x_peer)).wait_recv()
         merge(owner)
 
@@ -370,7 +365,7 @@
         pltpu.VMEM((tokens, columns), BF16),
         pltpu.VMEM((tokens, columns), BF16),
         dma((7,)),
-        dma((3,)), dma((3,)), dma((3, CHUNKS)), dma((3, CHUNKS)), dma((3,)), dma((3,)),
+        dma((3,)), dma((3,)), dma((3, UP_CHUNKS)), dma((3, UP_CHUNKS)), dma((3,)), dma((3,)),
         dma((CHUNKS, layers)), dma((CHUNKS, layers)),
         dma((CHUNKS, layers - 1)), dma((CHUNKS, layers - 1)),
         dma((CHUNKS, layers - 1)), dma((CHUNKS, layers - 1)),
@@ -443,7 +438,7 @@
 
     def on_device(*arrays):
         rows = arrays[5].shape[1]
-        if shards == 4 and reps % 2 == 0 and reps > 2 and rows % STRIP == 0:
+        if shards == 4 and reps % 2 == 0 and reps > 2 and rows % (CHUNKS * STRIP) == 0:
             return fused_call(reps, *arrays)
         return collective_form(*arrays)
 

time: 74.8 us -> 79 us (1.056)
  Pallas kernels: 74 us -> 78.2 us
    pallas_call x1, Pallas kernels: 72 us -> 76.2 us  [fused_call(): pl.pallas_call(functools.partial(fused, reps), out_shape=(pltpu.VMEM((tok...]
where the time goes in v5:
time: 79 us; the launch traced here: 78.9 us
  Pallas kernels  78.2 us (99%)
    pallas_call x1, Pallas kernels, fused_call(): pl.pallas_call(functools.partial(fused, reps), out_shape=(pltpu.VMEM((tok...  76.2 us
    pallas_call x1, Pallas kernels, fused_call(): pl.pallas_call(write_out, out_shape=tuple((jax.ShapeDtypeStruct((1,) + a....  2 us

profile of v5, /device:TPU:9, one launch (start us, length us, event | category | flops | bytes accessed | tf_op | source)
XLA Modules:
  0.0 78.9 jit_solution(5007019012622858589)
XLA Ops:
  0.6 76.2 %shard_map.102 = (bf16[256,1024]{1,0:T(8,128)(2,1)S(1)}, bf16[1152,1024]{1,0:T(8,128)(2,1)S(1)}, f32[144,1024]{1,0:T(8,128)S(1)}, f32[144,1024]{1,0:T(8,128)S(1)}) custom-call(bf16[1,256,4608]{2,1,0:T(8,128)(2,1)} %hidden.1, bf16[1,256,1024]{2,1,0:T(8,128)(2,1)} %upstream.1, bf16[1,1152,1024]{2,1,0:T(8,128)(2,1)} %weights.1, ...), custom_call_target="tpu_custom_call" | custom-call | flops 4831838208 | bytes 18874368 | tf_op jit(solution)/shard_map/pallas_call | solution.py:375
  76.9 2.0 %shard_map.103 = (bf16[1,256,1024]{2,1,0:T(8,128)(2,1)}, bf16[1,1152,1024]{2,1,0:T(8,128)(2,1)}, f32[1,144,1024]{2,1,0:T(8,128)}, f32[1,144,1024]{2,1,0:T(8,128)}) custom-call(bf16[256,1024]{1,0:T(8,128)(2,1)S(1)} %get-tuple-element.8.refs_0_, bf16[1152,1024]{1,0:T(8,128)(2,1)S(1)} %get-tuple-element.9.refs_1_, f32[144,1024]{1,0:T(8,128)S(1)} %get-tuple-element.10.refs_2_, ...), custom_call_target="tpu_custom_call" | custom-call | bytes 8388608 | tf_op jit(solution)/shard_map/pallas_call | solution.py:393

commit v6 on v4

--- a/solution.py
+++ b/solution.py
@@ -159,6 +159,8 @@
         send_piece(*piece)
     send_hidden(3)
     send_hidden(2)
+    for h in range(CHUNKS):
+        send_upstream(2, h)
     send_hidden(1)
     for h in range(CHUNKS):
         send_upstream(1, h)
@@ -268,15 +270,11 @@
     pairs(0)
     pairs(1)
     renew(0)
-    send_upstream(2, 0)
     pairs(2)
     renew(1)
-    send_upstream(2, 1)
     pairs(3)
     renew(2)
     forward(0)
-    send_upstream(2, 2)
-    send_upstream(2, 3)
     renew(3)
     forward(1)
 

time: 74.8 us -> 74.8 us (level)
  no operation moved by 1% of the time
where the time goes in v6:
time: 74.8 us; the launch traced here: 74.6 us
  Pallas kernels  74 us (99%)
    pallas_call x1, Pallas kernels, fused_call(): pl.pallas_call(functools.partial(fused, reps), out_shape=(pltpu.VMEM((tok...  72 us
    pallas_call x1, Pallas kernels, fused_call(): pl.pallas_call(write_out, out_shape=tuple((jax.ShapeDtypeStruct((1,) + a....  2 us

profile of v6, /device:TPU:9, one launch (start us, length us, event | category | flops | bytes accessed | tf_op | source)
XLA Modules:
  0.0 74.6 jit_solution(9337079710223921148)
XLA Ops:
  0.6 72.0 %shard_map.102 = (bf16[256,1024]{1,0:T(8,128)(2,1)S(1)}, bf16[1152,1024]{1,0:T(8,128)(2,1)S(1)}, f32[144,1024]{1,0:T(8,128)S(1)}, f32[144,1024]{1,0:T(8,128)S(1)}) custom-call(bf16[1,256,4608]{2,1,0:T(8,128)(2,1)} %hidden.1, bf16[1,256,1024]{2,1,0:T(8,128)(2,1)} %upstream.1, bf16[1,1152,1024]{2,1,0:T(8,128)(2,1)} %weights.1, ...), custom_call_target="tpu_custom_call" | custom-call | flops 4831838208 | bytes 18874368 | tf_op jit(solution)/shard_map/pallas_call | solution.py:378
  72.6 2.0 %shard_map.103 = (bf16[1,256,1024]{2,1,0:T(8,128)(2,1)}, bf16[1,1152,1024]{2,1,0:T(8,128)(2,1)}, f32[1,144,1024]{2,1,0:T(8,128)}, f32[1,144,1024]{2,1,0:T(8,128)}) custom-call(bf16[256,1024]{1,0:T(8,128)(2,1)S(1)} %get-tuple-element.8.refs_0_, bf16[1152,1024]{1,0:T(8,128)(2,1)S(1)} %get-tuple-element.9.refs_1_, f32[144,1024]{1,0:T(8,128)S(1)} %get-tuple-element.10.refs_2_, ...), custom_call_target="tpu_custom_call" | custom-call | bytes 8388608 | tf_op jit(solution)/shard_map/pallas_call | solution.py:396

commit v7 on v6

--- a/solution.py
+++ b/solution.py
@@ -273,14 +273,15 @@
     pairs(2)
     renew(1)
     pairs(3)
+    forward(0)
     renew(2)
-    forward(0)
-    renew(3)
-    forward(1)
 
     hidden_in(3)
     project(3, p_out.at[1])
     go(remote(p_out.at[1], p_in.at[1], p_send.at[1], p_recv.at[1], at_shard(sibling)))
+    turn(3)
+    renew(3)
+    forward(1)
     hidden_in(2)
     project(2, p_far)
     remote(p_in.at[1], p_in.at[1], p_send.at[1], p_recv.at[1], at_shard(sibling)).wait_recv()
@@ -292,15 +293,14 @@
     strips(tokens, chip_sum)
     go(remote(y_out, y_in, p_send.at[2], p_recv.at[2], at_shard(across)))
     forward(2)
-    turn(3)
     turn(2)
     loads[2].wait()
     loads[5].wait()
     loads[6].wait()
     pass_upstream(0)
     pass_upstream(1)
+    forward(3)
     inner(0)
-    forward(3)
     pass_upstream(2)
     inner(1)
     pass_upstream(3)

time: 74.8 us -> 76 us (1.016)
  the two profiles are of different devices: /device:TPU:9 before, /device:TPU:0 now
where the time goes in v7:
time: 76 us; the launch traced here: 75.8 us
  Pallas kernels  75.2 us (99%)
    pallas_call x1, Pallas kernels, fused_call(): pl.pallas_call(functools.partial(fused, reps), out_shape=(pltpu.VMEM((tok...  73.2 us
    pallas_call x1, Pallas kernels, fused_call(): pl.pallas_call(write_out, out_shape=tuple((jax.ShapeDtypeStruct((1,) + a....  2 us

profile of v7, /device:TPU:0, one launch (start us, length us, event | category | flops | bytes accessed | tf_op | source)
XLA Modules:
  0.0 75.8 jit_solution(13434042052444799315)
XLA Ops:
  0.6 73.2 %shard_map.102 = (bf16[256,1024]{1,0:T(8,128)(2,1)S(1)}, bf16[1152,1024]{1,0:T(8,128)(2,1)S(1)}, f32[144,1024]{1,0:T(8,128)S(1)}, f32[144,1024]{1,0:T(8,128)S(1)}) custom-call(bf16[1,256,4608]{2,1,0:T(8,128)(2,1)} %hidden.1, bf16[1,256,1024]{2,1,0:T(8,128)(2,1)} %upstream.1, bf16[1,1152,1024]{2,1,0:T(8,128)(2,1)} %weights.1, ...), custom_call_target="tpu_custom_call" | custom-call | flops 4831838208 | bytes 18874368 | tf_op jit(solution)/shard_map/pallas_call | solution.py:378
  73.8 2.0 %shard_map.103 = (bf16[1,256,1024]{2,1,0:T(8,128)(2,1)}, bf16[1,1152,1024]{2,1,0:T(8,128)(2,1)}, f32[1,144,1024]{2,1,0:T(8,128)}, f32[1,144,1024]{2,1,0:T(8,128)}) custom-call(bf16[256,1024]{1,0:T(8,128)(2,1)S(1)} %get-tuple-element.8.refs_0_, bf16[1152,1024]{1,0:T(8,128)(2,1)S(1)} %get-tuple-element.9.refs_1_, f32[144,1024]{1,0:T(8,128)S(1)} %get-tuple-element.10.refs_2_, ...), custom_call_target="tpu_custom_call" | custom-call | bytes 8388608 | tf_op jit(solution)/shard_map/pallas_call | solution.py:396
